TPU v7x, 32 devices: a whole 2x2x4 slice. The times are simulated.
32 devices in a mesh: dp: 4 (over y, x), row: 2 (over core), col: 4 (over z).
Axes of the slice: x: 2, y: 2, z: 4, core: 2. Of those that a mesh axis runs over, the one named last changes fastest.
Arguments:
- step_count: int32 [1], replicated, may hold values from 2 to 11
- ffn_weight: bfloat16 [4096, 10240], P('row', 'col'), may hold values from -40 to 40
- ffn_grads: float32 [4, 4096, 10240], P('dp', 'row', 'col'), may hold values from -80 to 80
- ffn_rows: float32 [4096], P('row'), may hold values from 0.1 to 12
- ffn_cols: float32 [10240], P('col'), may hold values from 0.1 to 1
- attn_weight: bfloat16 [4096, 4096], P('row', 'col'), may hold values from -40 to 40
- attn_grads: float32 [4, 4096, 4096], P('dp', 'row', 'col'), may hold values from -80 to 80
- attn_rows: float32 [4096], P('row'), may hold values from 0.1 to 12
- attn_cols: float32 [4096], P('col'), may hold values from 0.1 to 1
Outputs:
- ffn_weight_new: float32 [4096, 10240], P('row', 'col')
- ffn_update: float32 [4096, 10240], P('row', 'col')
- ffn_rows_new: float32 [4096], P('row')
- ffn_cols_new: float32 [10240], P('col')
- attn_weight_new: float32 [4096, 4096], P('row', 'col')
- attn_update: float32 [4096, 4096], P('row', 'col')
- attn_rows_new: float32 [4096], P('row')
- attn_cols_new: float32 [4096], P('col')
All inputs are finite; a program needn't handle non-finite values.
Results may differ from a plain program's by a relative error of at most 0.0003.
Values sent between devices are 32-bit elements; how exact they have to be, the bound alone decides.
A program may use at most 320 MiB of HBM per device.

v0:
```python
import jax
import jax.numpy as jnp
from jax import lax
from jax.sharding import PartitionSpec as P


def apply_step(w_tile, factor, update):
    return w_tile.astype(jnp.float32) - factor * update


def body(
    step_count,
    ffn_weight,
    ffn_grads,
    ffn_rows,
    ffn_cols,
    attn_weight,
    attn_grads,
    attn_rows,
    attn_cols,
):
    step_value = step_count[0].astype(jnp.float32)
    decay = 1.0 - step_value ** (-0.8)
    weights = (ffn_weight, attn_weight)
    rows_old = (ffn_rows, attn_rows)
    cols_old = (ffn_cols, attn_cols)
    row_devs = lax.axis_size("row")
    col_devs = lax.axis_size("col")
    widths_in = tuple((w_tile.shape[0] * row_devs for w_tile in weights))
    widths_out = tuple((w_tile.shape[1] * col_devs for w_tile in weights))
    summed = (
        lax.psum_scatter(ffn_grads[0], "dp", scatter_dimension=0, tiled=True),
        lax.psum_scatter(attn_grads[0], "dp", scatter_dimension=0, tiled=True),
    )
    share_rows = summed[0].shape[0]
    offset = lax.axis_index("dp") * share_rows
    owned_tiles = tuple(
        (lax.dynamic_slice_in_dim(w_tile, offset, share_rows, 0) for w_tile in weights)
    )
    squares = tuple((g_part * g_part + 1e-30 for g_part in summed))
    row_sums = lax.psum(tuple((jnp.sum(s_part, axis=1) for s_part in squares)), "col")
    col_part = tuple((jnp.sum(s_part, axis=0) for s_part in squares))
    row_full = lax.all_gather(row_sums, "dp", axis=0, tiled=True)
    col_sums = lax.psum(col_part, ("dp", "row"))
    rows_new = tuple(
        (
            decay * rows_old[index] + (1.0 - decay) * (row_full[index] / widths_out[index])
            for index in range(2)
        )
    )
    cols_new = tuple(
        (
            decay * cols_old[index] + (1.0 - decay) * (col_sums[index] / widths_in[index])
            for index in range(2)
        )
    )
    masses = lax.psum(tuple((jnp.sum(r_tile) for r_tile in rows_new)), "row")
    raw_updates = []
    update_sq = []
    for index in range(2):
        row_own = lax.dynamic_slice_in_dim(rows_new[index], offset, share_rows, 0)
        second = row_own[:, None] * cols_new[index][None, :] / (masses[index] / widths_in[index])
        raw_update = summed[index] / jnp.sqrt(second)
        raw_updates.append(raw_update)
        update_sq.append(jnp.sum(raw_update * raw_update))
    update_tot = lax.psum((update_sq[0], update_sq[1]), ("dp", "row", "col"))
    weight_tot = lax.psum(
        tuple((jnp.sum(jnp.square(w_tile.astype(jnp.float32))) for w_tile in weights)),
        ("row", "col"),
    )
    totals = tuple(update_tot) + tuple(weight_tot)
    clipped = []
    factors = []
    for index in range(2):
        entries = widths_in[index] * widths_out[index]
        update_rms = jnp.sqrt(totals[index] / entries)
        clipped.append(raw_updates[index] / jnp.maximum(1.0, update_rms))
        factors.append(0.01 * jnp.sqrt(totals[2 + index] / entries))
    quarter_new = [
        apply_step(owned_tiles[index], factors[index], clipped[index]) for index in range(2)
    ]
    fresh = (
        lax.all_gather(quarter_new[0], "dp", axis=0, tiled=True),
        lax.all_gather(quarter_new[1], "dp", axis=0, tiled=True),
    )
    clipped = (
        lax.all_gather(clipped[0], "dp", axis=0, tiled=True),
        lax.all_gather(clipped[1], "dp", axis=0, tiled=True),
    )
    return (
        fresh[0],
        clipped[0],
        rows_new[0],
        cols_new[0],
        fresh[1],
        clipped[1],
        rows_new[1],
        cols_new[1],
    )


def solution(mesh):
    in_specs = (
        P(),
        P("row", "col"),
        P("dp", "row", "col"),
        P("row"),
        P("col"),
        P("row", "col"),
        P("dp", "row", "col"),
        P("row"),
        P("col"),
    )
    out_specs = (
        P("row", "col"),
        P("row", "col"),
        P("row"),
        P("col"),
        P("row", "col"),
        P("row", "col"),
        P("row"),
        P("col"),
    )
    return jax.shard_map(body, mesh=mesh, in_specs=in_specs, out_specs=out_specs, check_vma=False)
```

profile of v0, /device:TPU:0, one launch (start us, length us, event | category | flops | bytes accessed | tf_op | source)
XLA Modules:
  0.0 1013.2 jit_solution(17527655425020090493)
XLA Ops:
  7.2 0.0 reduce-scatter.5.cloned.1.call-start
  7.2 0.7 reduce-scatter.5.cloned.1.call-update
  7.9 0.0 reduce-scatter.3.cloned.1.call-start
  7.9 0.7 reduce-scatter.3.cloned.1.call-update
  8.7 0.0 all-gather.11.cloned.1.call-start
  8.7 0.0 copy-start.3
  8.7 10.1 multiply_reduce_fusion
  18.8 0.0 copy-done.3
  18.8 0.0 copy-start.9
  18.8 0.0 copy-start.10
  18.8 0.0 copy-start.11
  18.8 0.0 copy-start.8
  18.9 2.8 multiply_reduce_fusion.1
  21.6 19.1 %all-reduce.1 = (f32[]{:T(128)}, f32[]{:T(128)}) all-reduce(f32[]{:T(128)} %multiply_reduce_fusion, f32[]{:T(128)} %multiply_reduce_fusion.1), channel_id=1, replica_groups=mesh['dp'=4,'row'=2,'col'=4] {'row','col'}, use_global_device_ids=true, to_apply=%region_1.0 | all-reduce | flops 2 | bytes 16 | tf_op jit(solution)/shard_map/psum | solution.py:67
  42.2 58.1 %reduce-scatter.5.cloned.1.call-done = f32[512,1024]{1,0:T(8,128)} async-done(((f32[2048,1024]{1,0:T(8,128)}), f32[512,1024]{1,0:T(8,128)}) %reduce-scatter.5.cloned.1.call-update) | async-done | bytes 2097168 | tf_op jit(solution)/shard_map/reduce_scatter | solution.py:33
  100.2 0.0 copy-start.1
  100.2 2.1 fusion.2
  102.4 189.1 %reduce-scatter.3.cloned.1.call-done = f32[512,2560]{1,0:T(8,128)} async-done(((f32[2048,2560]{1,0:T(8,128)}), f32[512,2560]{1,0:T(8,128)}) %reduce-scatter.3.cloned.1.call-update) | async-done | bytes 5242896 | tf_op jit(solution)/shard_map/reduce_scatter | solution.py:32
  291.4 3.4 fusion
  294.9 11.7 %all-reduce.3 = (f32[512]{0:T(512)S(1)}, f32[512]{0:T(512)S(1)}) all-reduce(f32[512]{0:T(512)S(1)} %get-tuple-element.9, f32[512]{0:T(512)S(1)} %get-tuple-element.11), channel_id=1, replica_groups=mesh['dp'=4,'row'=2,'col'=4] {'col'}, use_global_device_ids=true, to_apply=%region_4.0 | all-reduce | flops 1024 | bytes 8192 | tf_op jit(solution)/shard_map/psum | solution.py:41
  306.5 7.9 all-gather.1
  314.5 7.2 all-gather
  321.7 0.0 copy-done.9
  321.7 0.0 copy-done.10
  321.7 0.6 fusion.4
  322.3 0.0 copy-start.6
  322.3 3.1 all-reduce.4
  326.7 0.1 dynamic_slice.15
  326.8 0.1 dynamic_slice.13
  326.9 23.4 %all-reduce.2 = (f32[2560]{0:T(1024)S(1)}, f32[1024]{0:T(1024)S(1)}) all-reduce(f32[2560]{0:T(1024)S(1)} %get-tuple-element.8, f32[1024]{0:T(1024)S(1)} %get-tuple-element.10), channel_id=1, replica_groups=mesh['dp'=4,'row'=2,'col'=4] {'dp','row'}, use_global_device_ids=true, to_apply=%region_6.0 | all-reduce | flops 3584 | bytes 28672 | tf_op jit(solution)/shard_map/psum | solution.py:44
  350.2 0.0 copy-done.11
  350.3 0.0 copy-start.5
  350.3 0.0 copy-done.8
  350.3 0.0 copy-done.1
  350.3 0.0 copy-start.4
  350.3 1.5 multiply_reduce_fusion.3
  351.8 4.5 multiply_reduce_fusion.2
  356.3 37.1 %all-reduce = (f32[]{:T(128)}, f32[]{:T(128)}) all-reduce(f32[]{:T(128)} %multiply_reduce_fusion.2, f32[]{:T(128)} %multiply_reduce_fusion.3), channel_id=1, replica_groups=mesh['dp'=4,'row'=2,'col'=4] {'dp','row','col'}, use_global_device_ids=true, to_apply=%region_10.0 | all-reduce | flops 2 | bytes 16 | tf_op jit(solution)/shard_map/psum | solution.py:66
  394.1 3.9 multiply_subtract_fusion.1
  398.0 0.0 copy-done.6
  398.0 0.0 copy-done.7
  398.0 0.0 copy-done.5
  398.0 0.0 all-gather.11.cloned.1.call-update
  398.0 0.0 all-gather.13.cloned.1.call-start
  398.1 0.5 all-gather.13.cloned.1.call-update
  398.6 0.0 all-gather.7.cloned.1.call-start
  400.0 0.0 copy-done.4
  400.1 7.2 multiply_subtract_fusion
  407.3 0.0 all-gather.7.cloned.1.call-update
  407.3 0.0 all-gather.9.cloned.1.call-start
  407.3 0.5 all-gather.9.cloned.1.call-update
  407.9 79.4 %all-gather.11.cloned.1.call-done = f32[2048,1024]{1,0:T(8,128)} async-done(((f32[512,1024]{1,0:T(8,128)}), f32[2048,1024]{1,0:T(8,128)}) %all-gather.11.cloned.1.call-update) | async-done | bytes 8388624 | tf_op jit(solution)/shard_map/all_gather | solution.py:84
  487.3 89.9 %all-gather.13.cloned.1.call-done = f32[2048,1024]{1,0:T(8,128)} async-done(((f32[512,1024]{1,0:T(8,128)}), f32[2048,1024]{1,0:T(8,128)}) %all-gather.13.cloned.1.call-update) | async-done | bytes 8388624 | tf_op jit(solution)/shard_map/all_gather | solution.py:88
  577.2 195.5 %all-gather.7.cloned.1.call-done = f32[2048,2560]{1,0:T(8,128)} async-done(((f32[512,2560]{1,0:T(8,128)}), f32[2048,2560]{1,0:T(8,128)}) %all-gather.7.cloned.1.call-update) | async-done | bytes 20971536 | tf_op jit(solution)/shard_map/all_gather | solution.py:83
  772.7 195.5 %all-gather.9.cloned.1.call-done = f32[2048,2560]{1,0:T(8,128)} async-done(((f32[512,2560]{1,0:T(8,128)}), f32[2048,2560]{1,0:T(8,128)}) %all-gather.9.cloned.1.call-update) | async-done | bytes 20971536 | tf_op jit(solution)/shard_map/all_gather | solution.py:87
  968.2 0.0 copy-start
  968.2 18.0 %copy.22 = f32[2048,2560]{1,0:T(8,128)} copy(f32[2048,2560]{1,0:T(8,128)} %all-gather.7.cloned.1.call-done) | data formatting | bytes 41943040
  986.2 2.4 copy-done
  988.6 10.6 %copy.23 = f32[2048,2560]{1,0:T(8,128)} copy(f32[2048,2560]{1,0:T(8,128)S(1)} %copy-done) | data formatting | bytes 41943040
  999.3 0.0 copy-done.2
  999.3 3.6 copy.24
  1002.9 0.0 slice-done
  1002.9 0.1 slice-done.1
  1003.0 3.4 copy.25
  (9 shorter events, 0.0 us)
Async XLA Ops:
  7.2 93.0 %reduce-scatter.5.cloned.1.call-start = ((), (), s32[]{:S(2)}) async-start(), calls=%async_computation.5 | async-start | bytes 10485760 | tf_op jit(solution)/shard_map/reduce_scatter | solution.py:33
  7.9 283.5 %reduce-scatter.3.cloned.1.call-start = ((), (), s32[]{:S(2)}) async-start(), calls=%async_computation.2 | async-start | bytes 26214400 | tf_op jit(solution)/shard_map/reduce_scatter | solution.py:32
  8.7 478.6 %all-gather.11.cloned.1.call-start = ((), (), s32[]{:S(2)}) async-start(), calls=%async_computation.6 | async-start | bytes 10485760 | tf_op jit(solution)/shard_map/all_gather | solution.py:84
  8.7 10.1 %copy-start.3 = (bf16[2048,1024]{1,0:T(8,128)(2,1)S(1)}, bf16[2048,1024]{1,0:T(8,128)(2,1)}, u32[]{:S(2)}) copy-start(bf16[2048,1024]{1,0:T(8,128)(2,1)} %param.14) | copy-start | bytes 12582916
  18.8 302.9 %copy-start.9 = (f32[2048]{0:T(1024)S(1)}, f32[2048]{0:T(1024)}, u32[]{:S(2)}) copy-start(f32[2048]{0:T(1024)} %param.16) | copy-start | bytes 24580
  18.8 302.9 %copy-start.10 = (f32[2048]{0:T(1024)S(1)}, f32[2048]{0:T(1024)}, u32[]{:S(2)}) copy-start(f32[2048]{0:T(1024)} %param.12) | copy-start | bytes 24580
  18.8 331.4 %copy-start.11 = (f32[1024]{0:T(1024)S(1)}, f32[1024]{0:T(1024)}, u32[]{:S(2)}) copy-start(f32[1024]{0:T(1024)} %param.17) | copy-start | bytes 12292
  18.8 331.4 %copy-start.8 = (f32[2560]{0:T(1024)S(1)}, f32[2560]{0:T(1024)}, u32[]{:S(2)}) copy-start(f32[2560]{0:T(1024)} %param.13) | copy-start | bytes 30724
  100.2 250.1 %copy-start.1 = (f32[512,1024]{1,0:T(8,128)S(1)}, f32[512,1024]{1,0:T(8,128)}, u32[]{:S(2)}) copy-start(f32[512,1024]{1,0:T(8,128)} %reduce-scatter.5.cloned.1.call-done) | copy-start | bytes 6291460
  322.3 75.7 %copy-start.6 = (f32[2048]{0:T(1024)}, f32[2048]{0:T(1024)S(1)}, u32[]{:S(2)}) copy-start(f32[2048]{0:T(1024)S(1)} %get-tuple-element.46) | copy-start | bytes 24580
  322.3 75.7 %copy-start.7 = (f32[2048]{0:T(1024)}, f32[2048]{0:T(1024)S(1)}, u32[]{:S(2)}) copy-start(f32[2048]{0:T(1024)S(1)} %get-tuple-element.42) | copy-start | bytes 24580
  350.3 47.8 %copy-start.5 = (f32[1024]{0:T(1024)}, f32[1024]{0:T(1024)S(1)}, u32[]{:S(2)}) copy-start(f32[1024]{0:T(1024)S(1)} %multiply_add_fusion.5) | copy-start | bytes 12292
  350.3 49.7 %copy-start.4 = (f32[2560]{0:T(1024)}, f32[2560]{0:T(1024)S(1)}, u32[]{:S(2)}) copy-start(f32[2560]{0:T(1024)S(1)} %multiply_add_fusion.2) | copy-start | bytes 30724
  398.0 179.1 %all-gather.13.cloned.1.call-start = ((), (), s32[]{:S(2)}) async-start(), calls=%async_computation.7 | async-start | bytes 10485760 | tf_op jit(solution)/shard_map/all_gather | solution.py:88
  398.6 374.1 %all-gather.7.cloned.1.call-start = ((), (), s32[]{:S(2)}) async-start(), calls=%async_computation.3 | async-start | bytes 26214400 | tf_op jit(solution)/shard_map/all_gather | solution.py:83
  407.3 560.9 %all-gather.9.cloned.1.call-start = ((), (), s32[]{:S(2)}) async-start(), calls=%async_computation.4 | async-start | bytes 26214400 | tf_op jit(solution)/shard_map/all_gather | solution.py:87
  968.2 20.4 %copy-start = (f32[2048,2560]{1,0:T(8,128)S(1)}, f32[2048,2560]{1,0:T(8,128)}, u32[]{:S(2)}) copy-start(f32[2048,2560]{1,0:T(8,128)} %all-gather.9.cloned.1.call-done) | copy-start | bytes 62914564
  968.2 34.7 %slice-start = ((s8[8388608]{0:T(1024)(128)(4,1)}), s8[4194304]{0:T(1024)(128)(4,1)S(1)}, s32[]{:S(2)}) async-start(s8[8388608]{0:T(1024)(128)(4,1)} %bitcast.9), calls=%async_computation.8 | async-start | bytes 8388608
  988.6 10.6 %copy-start.2 = (f32[2048,1024]{1,0:T(8,128)S(1)}, f32[2048,1024]{1,0:T(8,128)}, u32[]{:S(2)}) copy-start(f32[2048,1024]{1,0:T(8,128)} %all-gather.11.cloned.1.call-done) | copy-start | bytes 25165828
  988.6 14.3 %slice-start.1 = ((s8[8388608]{0:T(1024)(128)(4,1)}), s8[4194304]{0:T(1024)(128)(4,1)S(1)}, s32[]{:S(2)}) async-start(s8[8388608]{0:T(1024)(128)(4,1)} %bitcast.9), calls=%async_computation.9 | async-start | bytes 8388608
Sparse Core Ops, SparseCore 0:
  11.1 89.0 reduce-scatter.4
  103.6 187.7 reduce-scatter.2
  398.2 89.0 all-gather.10
  489.5 87.5 all-gather.12
  579.5 193.1 all-gather.6
  775.0 193.1 all-gather.8
where the time goes:
time: 1010 us
  waiting for transfers between devices  810 us (80%)
  blocking collectives  110 us (11%)
  local copies, waits for them, and re-layouts  38.3 us (4%)
  other arithmetic  36.2 us (4%)
  between operations  19 us (2%)
    all_gather x1, waiting for transfers between devices, body(): lax.all_gather(clipped[0], 'dp', axis=0, tiled=True)  196 us
    all_gather x1, waiting for transfers between devices, body(): lax.all_gather(quarter_new[0], 'dp', axis=0, tiled=True)  196 us
    reduce_scatter x1, waiting for transfers between devices, body(): lax.psum_scatter(ffn_grads[0], 'dp', scatter_dimension=0, tiled=True)  189 us
    all_gather x1, waiting for transfers between devices, body(): lax.all_gather(clipped[1], 'dp', axis=0, tiled=True)  89.9 us
    all_gather x1, waiting for transfers between devices, body(): lax.all_gather(quarter_new[1], 'dp', axis=0, tiled=True)  79.4 us
    reduce_scatter x1, waiting for transfers between devices, body(): lax.psum_scatter(attn_grads[0], 'dp', scatter_dimension=0, tiled=True)  58.1 us
    unnamed x32, local copies, waits for them, and re-layouts  38.2 us
    psum x1, blocking collectives, body(): update_tot = lax.psum((update_sq[0], update_sq[1]), ('dp', 'row', 'col'))  37.1 us
  transfers between devices with their start and end apart: 6, of which 6 were waited for; matrix products, arithmetic and copies ran while one was open for 2% of the time, Pallas kernels for 0%

commit v1 on v0

--- a/solution.py
+++ b/solution.py
@@ -41,7 +41,7 @@
     row_sums = lax.psum(tuple((jnp.sum(s_part, axis=1) for s_part in squares)), "col")
     col_part = tuple((jnp.sum(s_part, axis=0) for s_part in squares))
     row_full = lax.all_gather(row_sums, "dp", axis=0, tiled=True)
-    col_sums = lax.psum(col_part, ("dp", "row"))
+    col_sums = lax.psum(lax.psum(col_part, "row"), "dp")
     rows_new = tuple(
         (
             decay * rows_old[index] + (1.0 - decay) * (row_full[index] / widths_out[index])

time: 1010 us -> 1010 us (level)
  no operation moved by 1% of the time
where the time goes in v1:
time: 1010 us
  waiting for transfers between devices  810 us (80%)
  blocking collectives  103 us (10%)
  local copies, waits for them, and re-layouts  38.3 us (4%)
  other arithmetic  36.2 us (4%)
  between operations  19 us (2%)
    all_gather x1, waiting for transfers between devices, body(): lax.all_gather(clipped[0], 'dp', axis=0, tiled=True)  196 us
    all_gather x1, waiting for transfers between devices, body(): lax.all_gather(quarter_new[0], 'dp', axis=0, tiled=True)  196 us
    reduce_scatter x1, waiting for transfers between devices, body(): lax.psum_scatter(ffn_grads[0], 'dp', scatter_dimension=0, tiled=True)  189 us
    all_gather x1, waiting for transfers between devices, body(): lax.all_gather(clipped[1], 'dp', axis=0, tiled=True)  89.9 us
    all_gather x1, waiting for transfers between devices, body(): lax.all_gather(quarter_new[1], 'dp', axis=0, tiled=True)  79.4 us
    reduce_scatter x1, waiting for transfers between devices, body(): lax.psum_scatter(attn_grads[0], 'dp', scatter_dimension=0, tiled=True)  58.1 us
    unnamed x32, local copies, waits for them, and re-layouts  38.2 us
    psum x1, blocking collectives, body(): update_tot = lax.psum((update_sq[0], update_sq[1]), ('dp', 'row', 'col'))  37.1 us
  transfers between devices with their start and end apart: 6, of which 6 were waited for; matrix products, arithmetic and copies ran while one was open for 2% of the time, Pallas kernels for 0%

profile of v1, /device:TPU:0, one launch (start us, length us, event | category | flops | bytes accessed | tf_op | source)
XLA Modules:
  0.0 1006.3 jit_solution(1410422167678306964)
XLA Ops:
  7.2 0.0 reduce-scatter.5.cloned.1.call-start
  7.2 0.7 reduce-scatter.5.cloned.1.call-update
  7.9 0.0 reduce-scatter.3.cloned.1.call-start
  7.9 0.7 reduce-scatter.3.cloned.1.call-update
  8.7 0.0 all-gather.11.cloned.1.call-start
  8.7 0.0 copy-start.3
  8.7 10.1 %multiply_reduce_fusion = f32[]{:T(128)} fusion(bf16[2048,2560]{1,0:T(8,128)(2,1)} %param.10), kind=kLoop, calls=%fused_computation | loop fusion | flops 15728639 | bytes 10485764 | tf_op jit(solution)/shard_map/reduce_sum | solution.py:68
  18.8 0.0 copy-done.3
  18.8 0.0 copy-start.9
  18.8 0.0 copy-start.10
  18.8 0.0 copy-start.11
  18.8 0.0 copy-start.8
  18.9 2.8 multiply_reduce_fusion.1
  21.6 19.1 %all-reduce.1 = (f32[]{:T(128)}, f32[]{:T(128)}) all-reduce(f32[]{:T(128)} %multiply_reduce_fusion, f32[]{:T(128)} %multiply_reduce_fusion.1), channel_id=1, replica_groups=mesh['dp'=4,'row'=2,'col'=4] {'row','col'}, use_global_device_ids=true, to_apply=%region_1.0 | all-reduce | flops 2 | bytes 16 | tf_op jit(solution)/shard_map/psum | solution.py:67
  42.2 58.1 %reduce-scatter.5.cloned.1.call-done = f32[512,1024]{1,0:T(8,128)} async-done(((f32[2048,1024]{1,0:T(8,128)}), f32[512,1024]{1,0:T(8,128)}) %reduce-scatter.5.cloned.1.call-update) | async-done | bytes 2097168 | tf_op jit(solution)/shard_map/reduce_scatter | solution.py:33
  100.2 0.0 copy-start.1
  100.2 2.1 fusion.2
  102.4 189.1 %reduce-scatter.3.cloned.1.call-done = f32[512,2560]{1,0:T(8,128)} async-done(((f32[2048,2560]{1,0:T(8,128)}), f32[512,2560]{1,0:T(8,128)}) %reduce-scatter.3.cloned.1.call-update) | async-done | bytes 5242896 | tf_op jit(solution)/shard_map/reduce_scatter | solution.py:32
  291.4 3.4 fusion
  294.9 11.7 %all-reduce.2 = (f32[512]{0:T(512)S(1)}, f32[512]{0:T(512)S(1)}) all-reduce(f32[512]{0:T(512)S(1)} %get-tuple-element.9, f32[512]{0:T(512)S(1)} %get-tuple-element.11), channel_id=1, replica_groups=mesh['dp'=4,'row'=2,'col'=4] {'col'}, use_global_device_ids=true, to_apply=%region_4.0 | all-reduce | flops 1024 | bytes 8192 | tf_op jit(solution)/shard_map/psum | solution.py:41
  306.5 7.9 all-gather.1
  314.5 7.2 all-gather
  321.7 0.0 copy-done.9
  321.7 0.0 copy-done.10
  321.7 0.6 fusion.4
  322.3 0.0 copy-start.6
  322.3 4.5 all-reduce.4
  328.1 0.1 dynamic_slice.15
  328.2 0.1 dynamic_slice.13
  328.3 15.1 %all-reduce.3 = (f32[2560]{0:T(1024)S(1)}, f32[1024]{0:T(1024)S(1)}) all-reduce(f32[2560]{0:T(1024)S(1)} %get-tuple-element.21, f32[1024]{0:T(1024)S(1)} %get-tuple-element.22), channel_id=1, replica_groups=mesh['dp'=4,'row'=2,'col'=4] {'dp'}, use_global_device_ids=true, to_apply=%region_7.0 | all-reduce | flops 3584 | bytes 28672 | tf_op jit(solution)/shard_map/psum | solution.py:44
  343.3 0.0 copy-done.11
  343.3 0.0 copy-start.5
  343.4 0.0 copy-done.8
  343.4 0.0 copy-done.1
  343.4 0.0 copy-start.4
  343.4 1.5 multiply_reduce_fusion.3
  344.9 4.5 multiply_reduce_fusion.2
  349.4 37.1 %all-reduce = (f32[]{:T(128)}, f32[]{:T(128)}) all-reduce(f32[]{:T(128)} %multiply_reduce_fusion.2, f32[]{:T(128)} %multiply_reduce_fusion.3), channel_id=1, replica_groups=mesh['dp'=4,'row'=2,'col'=4] {'dp','row','col'}, use_global_device_ids=true, to_apply=%region_11.0 | all-reduce | flops 2 | bytes 16 | tf_op jit(solution)/shard_map/psum | solution.py:66
  387.2 3.9 multiply_subtract_fusion.1
  391.1 0.0 copy-done.6
  391.1 0.0 copy-done.7
  391.1 0.0 copy-done.5
  391.1 0.0 all-gather.11.cloned.1.call-update
  391.1 0.0 all-gather.13.cloned.1.call-start
  391.2 0.5 all-gather.13.cloned.1.call-update
  391.7 0.0 all-gather.7.cloned.1.call-start
  393.1 0.0 copy-done.4
  393.1 7.2 multiply_subtract_fusion
  400.4 0.0 all-gather.7.cloned.1.call-update
  400.4 0.0 all-gather.9.cloned.1.call-start
  400.4 0.5 all-gather.9.cloned.1.call-update
  401.0 79.4 %all-gather.11.cloned.1.call-done = f32[2048,1024]{1,0:T(8,128)} async-done(((f32[512,1024]{1,0:T(8,128)}), f32[2048,1024]{1,0:T(8,128)}) %all-gather.11.cloned.1.call-update) | async-done | bytes 8388624 | tf_op jit(solution)/shard_map/all_gather | solution.py:84
  480.3 89.9 %all-gather.13.cloned.1.call-done = f32[2048,1024]{1,0:T(8,128)} async-done(((f32[512,1024]{1,0:T(8,128)}), f32[2048,1024]{1,0:T(8,128)}) %all-gather.13.cloned.1.call-update) | async-done | bytes 8388624 | tf_op jit(solution)/shard_map/all_gather | solution.py:88
  570.3 195.5 %all-gather.7.cloned.1.call-done = f32[2048,2560]{1,0:T(8,128)} async-done(((f32[512,2560]{1,0:T(8,128)}), f32[2048,2560]{1,0:T(8,128)}) %all-gather.7.cloned.1.call-update) | async-done | bytes 20971536 | tf_op jit(solution)/shard_map/all_gather | solution.py:83
  765.8 195.5 %all-gather.9.cloned.1.call-done = f32[2048,2560]{1,0:T(8,128)} async-done(((f32[512,2560]{1,0:T(8,128)}), f32[2048,2560]{1,0:T(8,128)}) %all-gather.9.cloned.1.call-update) | async-done | bytes 20971536 | tf_op jit(solution)/shard_map/all_gather | solution.py:87
  961.3 0.0 copy-start
  961.3 18.0 %copy.22 = f32[2048,2560]{1,0:T(8,128)} copy(f32[2048,2560]{1,0:T(8,128)} %all-gather.7.cloned.1.call-done) | data formatting | bytes 41943040
  979.3 2.4 copy-done
  981.7 10.6 %copy.23 = f32[2048,2560]{1,0:T(8,128)} copy(f32[2048,2560]{1,0:T(8,128)S(1)} %copy-done) | data formatting | bytes 41943040
  992.3 0.0 copy-done.2
  992.3 3.6 copy.24
  996.0 0.0 slice-done
  996.0 0.1 slice-done.1
  996.1 3.4 copy.25
  (9 shorter events, 0.0 us)
Async XLA Ops:
  7.2 93.0 %reduce-scatter.5.cloned.1.call-start = ((), (), s32[]{:S(2)}) async-start(), calls=%async_computation.5 | async-start | bytes 10485760 | tf_op jit(solution)/shard_map/reduce_scatter | solution.py:33
  7.9 283.5 %reduce-scatter.3.cloned.1.call-start = ((), (), s32[]{:S(2)}) async-start(), calls=%async_computation.2 | async-start | bytes 26214400 | tf_op jit(solution)/shard_map/reduce_scatter | solution.py:32
  8.7 471.7 %all-gather.11.cloned.1.call-start = ((), (), s32[]{:S(2)}) async-start(), calls=%async_computation.6 | async-start | bytes 10485760 | tf_op jit(solution)/shard_map/all_gather | solution.py:84
  8.7 10.1 %copy-start.3 = (bf16[2048,1024]{1,0:T(8,128)(2,1)S(1)}, bf16[2048,1024]{1,0:T(8,128)(2,1)}, u32[]{:S(2)}) copy-start(bf16[2048,1024]{1,0:T(8,128)(2,1)} %param.14) | copy-start | bytes 12582916
  18.8 302.9 %copy-start.9 = (f32[2048]{0:T(1024)S(1)}, f32[2048]{0:T(1024)}, u32[]{:S(2)}) copy-start(f32[2048]{0:T(1024)} %param.16) | copy-start | bytes 24580
  18.8 302.9 %copy-start.10 = (f32[2048]{0:T(1024)S(1)}, f32[2048]{0:T(1024)}, u32[]{:S(2)}) copy-start(f32[2048]{0:T(1024)} %param.12) | copy-start | bytes 24580
  18.8 324.5 %copy-start.11 = (f32[1024]{0:T(1024)S(1)}, f32[1024]{0:T(1024)}, u32[]{:S(2)}) copy-start(f32[1024]{0:T(1024)} %param.17) | copy-start | bytes 12292
  18.8 324.5 %copy-start.8 = (f32[2560]{0:T(1024)S(1)}, f32[2560]{0:T(1024)}, u32[]{:S(2)}) copy-start(f32[2560]{0:T(1024)} %param.13) | copy-start | bytes 30724
  100.2 243.2 %copy-start.1 = (f32[512,1024]{1,0:T(8,128)S(1)}, f32[512,1024]{1,0:T(8,128)}, u32[]{:S(2)}) copy-start(f32[512,1024]{1,0:T(8,128)} %reduce-scatter.5.cloned.1.call-done) | copy-start | bytes 6291460
  322.3 68.8 %copy-start.6 = (f32[2048]{0:T(1024)}, f32[2048]{0:T(1024)S(1)}, u32[]{:S(2)}) copy-start(f32[2048]{0:T(1024)S(1)} %get-tuple-element.48) | copy-start | bytes 24580
  322.3 68.8 %copy-start.7 = (f32[2048]{0:T(1024)}, f32[2048]{0:T(1024)S(1)}, u32[]{:S(2)}) copy-start(f32[2048]{0:T(1024)S(1)} %get-tuple-element.44) | copy-start | bytes 24580
  343.3 47.8 %copy-start.5 = (f32[1024]{0:T(1024)}, f32[1024]{0:T(1024)S(1)}, u32[]{:S(2)}) copy-start(f32[1024]{0:T(1024)S(1)} %multiply_add_fusion.5) | copy-start | bytes 12292
  343.4 49.7 %copy-start.4 = (f32[2560]{0:T(1024)}, f32[2560]{0:T(1024)S(1)}, u32[]{:S(2)}) copy-start(f32[2560]{0:T(1024)S(1)} %multiply_add_fusion.2) | copy-start | bytes 30724
  391.1 179.1 %all-gather.13.cloned.1.call-start = ((), (), s32[]{:S(2)}) async-start(), calls=%async_computation.7 | async-start | bytes 10485760 | tf_op jit(solution)/shard_map/all_gather | solution.py:88
  391.7 374.1 %all-gather.7.cloned.1.call-start = ((), (), s32[]{:S(2)}) async-start(), calls=%async_computation.3 | async-start | bytes 26214400 | tf_op jit(solution)/shard_map/all_gather | solution.py:83
  400.4 560.9 %all-gather.9.cloned.1.call-start = ((), (), s32[]{:S(2)}) async-start(), calls=%async_computation.4 | async-start | bytes 26214400 | tf_op jit(solution)/shard_map/all_gather | solution.py:87
  961.3 20.4 %copy-start = (f32[2048,2560]{1,0:T(8,128)S(1)}, f32[2048,2560]{1,0:T(8,128)}, u32[]{:S(2)}) copy-start(f32[2048,2560]{1,0:T(8,128)} %all-gather.9.cloned.1.call-done) | copy-start | bytes 62914564
  961.3 34.7 %slice-start = ((s8[8388608]{0:T(1024)(128)(4,1)}), s8[4194304]{0:T(1024)(128)(4,1)S(1)}, s32[]{:S(2)}) async-start(s8[8388608]{0:T(1024)(128)(4,1)} %bitcast.9), calls=%async_computation.8 | async-start | bytes 8388608
  981.7 10.6 %copy-start.2 = (f32[2048,1024]{1,0:T(8,128)S(1)}, f32[2048,1024]{1,0:T(8,128)}, u32[]{:S(2)}) copy-start(f32[2048,1024]{1,0:T(8,128)} %all-gather.11.cloned.1.call-done) | copy-start | bytes 25165828
  981.7 14.3 %slice-start.1 = ((s8[8388608]{0:T(1024)(128)(4,1)}), s8[4194304]{0:T(1024)(128)(4,1)S(1)}, s32[]{:S(2)}) async-start(s8[8388608]{0:T(1024)(128)(4,1)} %bitcast.9), calls=%async_computation.9 | async-start | bytes 8388608
Sparse Core Ops, SparseCore 0:
  11.1 89.0 reduce-scatter.4
  103.6 187.7 reduce-scatter.2
  391.2 89.0 all-gather.10
  482.6 87.5 all-gather.12
  572.6 193.1 all-gather.6
  768.1 193.1 all-gather.8
